TPU v7x, 256 devices: a whole 4x4x8 slice. The times are simulated.
256 devices in a mesh: tm: 64 (over y, z_hi, x), chan: 4 (over z_lo, core).
Axes of the slice: x: 4, y: 4, z: 8 (z_hi: 4, z_lo: 2; z = z_hi * 2 + z_lo), core: 2. Of those that a mesh axis runs over, the one named last changes fastest.
Arguments:
- latents: bfloat16 [512, 256, 512], P('chan', 'tm'), may hold values from -6 to 6
- conv_weight: bfloat16 [512, 3, 9, 512], P(None, None, None, 'chan'), may hold values from -0.0546875 to 0.0546875
- norm_gain: float32 [512], P('chan'), may hold values from 0.1 to 1.9
- norm_bias: float32 [512], P('chan'), may hold values from -3 to 3
- clip_lengths: int32 [12], replicated, may hold values from 1 to 64, 256 in all
- slab_bounds: int32 [64, 2], P('tm'), may hold values from 0 to 256, as said below
Outputs:
- decoded: bfloat16 [512, 512, 512], P('chan', 'tm')
Inputs may be any that keep to these rules, and one draw needn't show every extreme that they name: `clip_lengths`: the clips lie end to end and cover all 256 frames; the longest clip has exactly a quarter of 256 frames. `slab_bounds`: slab 0 starts at frame 0, the last slab ends at 256, each slab ends where the next starts, slab s starts within 2 frames of s * 4, so a slab holds 0 to 8 frames; some slab holds exactly 8 frames.
All inputs are finite; a program needn't handle non-finite values.
Results may differ from a plain program's by a relative error of at most 0.001.
Values may be sent and summed in bfloat16 or wider, within the bound.
A program may use at most 128 MiB of HBM per device.

v0:
```python
import jax
import jax.numpy as jnp
from jax import lax
from jax.sharding import PartitionSpec as P

C = 512
GROUPS = 32
H = 16
W = 32


norm_eps = 1e-06


def padded_2(block, sides, width):
    for axis, dim in sides:
        count = lax.axis_size(axis)
        forward = [(i, i + 1) for i in range(count - 1)]
        backward = [(target, source) for source, target in forward]
        low = lax.ppermute(
            lax.slice_in_dim(block, block.shape[dim] - width, None, axis=dim), axis, forward
        )
        high = lax.ppermute(lax.slice_in_dim(block, 0, width, axis=dim), axis, backward)
        block = jnp.concatenate([low, block, high], axis=dim)
    return block


def frame_starts(clip_lengths, frames):
    clip_ends = jnp.cumsum(clip_lengths)
    starts = clip_ends - clip_lengths
    chosen = jnp.where(starts[None, :] <= frames[:, None], starts[None, :], 0)
    return jnp.max(chosen, axis=1)


def tap_sources(frames, clip_lengths):
    clip_first = frame_starts(clip_lengths, frames)
    return jnp.stack([jnp.maximum(frames - 2 + offset, clip_first) for offset in range(3)])


def columns(extended, local_index):
    channels = extended.shape[0]
    frame_count = local_index.shape[0]
    picked = jnp.take(extended, local_index, axis=1).reshape(channels, frame_count, H, W)
    padded = jnp.pad(picked, ((0, 0), (0, 0), (1, 1), (1, 1)))
    pieces = [
        padded[:, :, row_tap : row_tap + H, col_tap : col_tap + W]
        for row_tap in range(3)
        for col_tap in range(3)
    ]
    return jnp.stack(pieces).reshape(9 * channels, frame_count * H * W)


def norm_block(summed, residual, norm_gain, norm_bias):
    channels, frame_count, cell_count = summed.shape
    group_width = C // GROUPS
    grouped = summed.reshape(channels // group_width, group_width, frame_count, cell_count)
    average = jnp.mean(grouped, axis=(1, 3), keepdims=True)
    variance = jnp.mean(jnp.square(grouped - average), axis=(1, 3), keepdims=True)
    normed = ((grouped - average) * lax.rsqrt(variance + norm_eps)).reshape(
        channels, frame_count, cell_count
    )
    normed = normed * norm_gain[:, None, None] + norm_bias[:, None, None]
    return (jax.nn.silu(normed) + residual.astype(jnp.float32)).astype(jnp.bfloat16)


def shards(latents, conv_weight, norm_gain, norm_bias, clip_lengths, slab_bounds):
    channels, frame_count, cell_count = latents.shape
    out_channels = conv_weight.shape[0]
    own_rows = out_channels // lax.axis_size("chan")
    capacity = 2 * frame_count
    slab_index = lax.axis_index("tm")
    slab_first = slab_bounds[0, 0]
    slab_end = slab_bounds[0, 1]
    slot_index = jnp.arange(capacity, dtype=jnp.int32)
    occupied = slot_index < slab_end - slab_first
    wanted = jnp.where(occupied, slab_first + slot_index, slab_first)
    weights = [conv_weight[:, offset].reshape(out_channels, 9 * channels) for offset in range(3)]
    extended = padded_2(latents, (("tm", 1),), frame_count)
    anchor = (slab_index - 1) * frame_count
    sources = tap_sources(wanted, clip_lengths) - anchor
    stacks = [columns(extended, sources[offset]) for offset in range(3)]
    summed = jnp.zeros((own_rows * lax.axis_size("chan"), stacks[0].shape[1]), jnp.float32)
    for offset in range(3):
        weight_rows = weights[offset]
        summed = summed + jnp.dot(weight_rows, stacks[offset], preferred_element_type=jnp.float32)
    partial_total = lax.psum_scatter(summed, "chan", scatter_dimension=0, tiled=True)
    residual = jnp.take(extended, wanted - anchor, axis=1)
    decoded = norm_block(
        partial_total.reshape(own_rows, wanted.shape[0], cell_count), residual, norm_gain, norm_bias
    )
    return jnp.where(occupied[None, :, None], decoded, jnp.zeros_like(decoded))


def solution(mesh):
    placed = (
        P("chan", "tm", None),
        P(None, None, None, "chan"),
        P("chan"),
        P("chan"),
        P(),
        P("tm", None),
    )
    return jax.shard_map(
        shards, mesh=mesh, in_specs=placed, out_specs=P("chan", "tm", None), check_vma=False
    )
```

profile of v0, /device:TPU:56, one launch (start us, length us, event | category | flops | bytes accessed | tf_op | source)
XLA Modules:
  0.0 238.7 jit_solution(4429731119021834983)
XLA Ops:
  6.5 1.9 copy.30
  8.5 3.4 %collective-permute-start = (bf16[128,4,512]{2,0,1:T(8,128)(2,1)}, bf16[128,4,512]{2,0,1:T(8,128)(2,1)}, u32[]{:S(2)}, u32[]{:S(2)}) collective-permute-start(bf16[128,4,512]{2,0,1:T(8,128)(2,1)} %copy.30), channel_id=1, source_target_pairs={{0,4},{4,8},{8,12},{12,16},{16,20},{20,24},{24,28},{28,32},{32,36}... | collective-permute-start | bytes 1572872 | tf_op jit(solution)/shard_map/ppermute | solution.py:20
  11.9 8.2 %collective-permute-start.1 = (bf16[128,4,512]{2,0,1:T(8,128)(2,1)}, bf16[128,4,512]{2,0,1:T(8,128)(2,1)}, u32[]{:S(2)}, u32[]{:S(2)}) collective-permute-start(bf16[128,4,512]{2,0,1:T(8,128)(2,1)} %copy.30), channel_id=1, source_target_pairs={{4,0},{8,4},{12,8},{16,12},{20,16},{24,20},{28,24},{32,28},{36,32}... | collective-permute-start | bytes 1572872 | tf_op jit(solution)/shard_map/ppermute | solution.py:23
  20.1 1.3 fusion.62
  26.9 2.2 fusion.61
  29.1 1.4 copy.52
  30.6 1.4 copy.51
  32.0 1.5 copy.50
  34.2 7.4 %collective-permute-done = bf16[128,4,512]{2,0,1:T(8,128)(2,1)} collective-permute-done((bf16[128,4,512]{2,0,1:T(8,128)(2,1)}, bf16[128,4,512]{2,0,1:T(8,128)(2,1)}, u32[]{:S(2)}, u32[]{:S(2)}) %collective-permute-start) | collective-permute-done | bytes 524320 | tf_op jit(solution)/shard_map/ppermute | solution.py:20
  46.7 1.6 copy.41
  51.8 11.4 %copy.43 = bf16[9,128,8,16,32]{1,0,4,3,2:T(8,128)(2,1)} copy(bf16[9,128,8,16,32]{1,4,3,2,0:T(8,128)(2,1)S(1)} %fusion.60) | data formatting | bytes 18874368 | tf_op jit(solution)/shard_map/stack | solution.py:50
  64.9 1.6 copy.37
  70.0 11.4 %copy.39 = bf16[9,128,8,16,32]{1,0,4,3,2:T(8,128)(2,1)} copy(bf16[9,128,8,16,32]{1,4,3,2,0:T(8,128)(2,1)S(1)} %fusion.44) | data formatting | bytes 18874368 | tf_op jit(solution)/shard_map/stack | solution.py:50
  83.1 1.8 copy.33
  88.4 11.4 %copy.35 = bf16[9,128,8,16,32]{1,0,4,3,2:T(8,128)(2,1)} copy(bf16[9,128,8,16,32]{1,4,3,2,0:T(8,128)(2,1)S(1)} %fusion.28) | data formatting | bytes 18874368 | tf_op jit(solution)/shard_map/stack | solution.py:50
  99.8 8.1 %fusion = f32[4096,512]{1,0:T(8,128)} fusion(bf16[512,1152]{0,1:T(8,128)(2,1)S(1)} %bitcast.215, bf16[512,8,9,128]{3,2,1,0:T(8,128)(2,1)S(1)} %bitcast.208), kind=kOutput, calls=%fused_computation.4 | convolution fusion | flops 4831838208 | bytes 19005440 | tf_op jit(solution)/shard_map/dot_general | solution.py:85
  107.9 14.0 %fusion.3 = f32[4096,512]{1,0:T(8,128)} fusion(bf16[512,1152]{0,1:T(8,128)(2,1)S(1)} %bitcast.213, bf16[512,8,9,128]{3,2,1,0:T(8,128)(2,1)} %bitcast.209), kind=kOutput, calls=%fused_computation.7 | convolution fusion | flops 4831838208 | bytes 19005440 | tf_op jit(solution)/shard_map/dot_general | solution.py:85
  121.9 17.1 %add_bitcast_fusion = f32[512,4096]{0,1:T(8,128)} fusion(f32[4096,512]{1,0:T(8,128)} %fusion, f32[4096,512]{1,0:T(8,128)} %fusion.3, bf16[512,1152]{0,1:T(8,128)(2,1)S(1)} %bitcast.214, bf16[512,8,9,128]{3,2,1,0:T(8,128)(2,1)} %bitcast.210), kind=kOutput, calls=%fused_computation.13 | convolution fusion | flops 4836032512 | bytes 35782656 | tf_op jit(solution)/shard_map/dot_general | solution.py:85
  139.1 1.6 gather_fusion.3
  140.7 79.2 %reduce-scatter.2.cloned.1.call-done = f32[128,4096]{0,1:T(8,128)} async-done(((f32[512,4096]{0,1:T(8,128)}), f32[128,4096]{0,1:T(8,128)}) %reduce-scatter.2.cloned.1.call-update) | async-done | bytes 2097168 | tf_op jit(solution)/shard_map/reduce_scatter | solution.py:86
  219.9 2.9 %copy.45 = f32[128,4096]{1,0:T(8,128)} copy(f32[128,4096]{0,1:T(8,128)} %reduce-scatter.2.cloned.1.call-done) | data formatting | bytes 4194304 | tf_op jit(solution)/shard_map/reduce_scatter | solution.py:86
  222.8 3.2 %copy.56 = f32[16,8,8,512]{3,2,1,0:T(8,128)S(1)} copy(f32[16,8,8,512]{3,1,2,0:T(8,128)} %bitcast.212) | data formatting | bytes 4194304
  227.0 1.9 copy.47
  230.3 1.5 copy.49
  (86 shorter events, 26.0 us)
Async XLA Ops:
  6.5 213.4 %reduce-scatter.2.cloned.1.call-start = ((), (), s32[]{:S(2)}) async-start(), calls=%async_computation.1 | async-start | bytes 10485760 | tf_op jit(solution)/shard_map/reduce_scatter | solution.py:86
  8.5 33.1 %collective-permute-start = (bf16[128,4,512]{2,0,1:T(8,128)(2,1)}, bf16[128,4,512]{2,0,1:T(8,128)(2,1)}, u32[]{:S(2)}, u32[]{:S(2)}) collective-permute-start(bf16[128,4,512]{2,0,1:T(8,128)(2,1)} %copy.30), channel_id=1, source_target_pairs={{0,4},{4,8},{8,12},{12,16},{16,20},{20,24},{24,28},{28,32},{32,36}... | collective-permute-start | bytes 1572872 | tf_op jit(solution)/shard_map/ppermute | solution.py:20
  11.9 32.0 %collective-permute-start.1 = (bf16[128,4,512]{2,0,1:T(8,128)(2,1)}, bf16[128,4,512]{2,0,1:T(8,128)(2,1)}, u32[]{:S(2)}, u32[]{:S(2)}) collective-permute-start(bf16[128,4,512]{2,0,1:T(8,128)(2,1)} %copy.30), channel_id=1, source_target_pairs={{4,0},{8,4},{12,8},{16,12},{20,16},{24,20},{28,24},{32,28},{36,32}... | collective-permute-start | bytes 1572872 | tf_op jit(solution)/shard_map/ppermute | solution.py:23
  87.6 12.1 %slice-start = ((s8[16777216]{0:T(1024)(128)(4,1)}), s8[4194304]{0:T(1024)(128)(4,1)S(1)}, s32[]{:S(2)}) async-start(s8[16777216]{0:T(1024)(128)(4,1)} %bitcast.206), calls=%async_computation.2 | async-start | bytes 8388608
  88.3 11.4 %slice-start.1 = ((s8[16777216]{0:T(1024)(128)(4,1)}), s8[4194304]{0:T(1024)(128)(4,1)S(1)}, s32[]{:S(2)}) async-start(s8[16777216]{0:T(1024)(128)(4,1)} %bitcast.206), calls=%async_computation.3 | async-start | bytes 8388608
  88.3 11.4 %slice-start.2 = ((s8[16777216]{0:T(1024)(128)(4,1)}), s8[4194304]{0:T(1024)(128)(4,1)S(1)}, s32[]{:S(2)}) async-start(s8[16777216]{0:T(1024)(128)(4,1)} %bitcast.206), calls=%async_computation.4 | async-start | bytes 8388608
  88.4 11.4 %slice-start.3 = ((s8[16777216]{0:T(1024)(128)(4,1)}), s8[4194304]{0:T(1024)(128)(4,1)S(1)}, s32[]{:S(2)}) async-start(s8[16777216]{0:T(1024)(128)(4,1)} %bitcast.206), calls=%async_computation.5 | async-start | bytes 8388608
  88.4 11.4 %copy-start.3 = (bf16[512,1,9,128]{0,3,2,1:T(8,128)(2,1)S(1)}, bf16[512,1,9,128]{0,3,2,1:T(8,128)(2,1)}, u32[]{:S(2)}) copy-start(bf16[512,1,9,128]{0,3,2,1:T(8,128)(2,1)} %copy.52) | copy-start | bytes 3538948
  99.8 8.1 %copy-start.1 = (bf16[512,1,9,128]{0,3,2,1:T(8,128)(2,1)S(1)}, bf16[512,1,9,128]{0,3,2,1:T(8,128)(2,1)}, u32[]{:S(2)}) copy-start(bf16[512,1,9,128]{0,3,2,1:T(8,128)(2,1)} %copy.51) | copy-start | bytes 3538948
  107.9 14.0 %copy-start.2 = (bf16[512,1,9,128]{0,3,2,1:T(8,128)(2,1)S(1)}, bf16[512,1,9,128]{0,3,2,1:T(8,128)(2,1)}, u32[]{:S(2)}) copy-start(bf16[512,1,9,128]{0,3,2,1:T(8,128)(2,1)} %copy.50) | copy-start | bytes 3538948
  121.9 17.2 %copy-start.4 = (s32[8]{0:T(128)S(1)}, s32[8]{0:T(128)}, u32[]{:S(2)}) copy-start(s32[8]{0:T(128)} %get-tuple-element.13) | copy-start | bytes 100
  139.1 90.0 %copy-start.5 = (pred[8]{0:T(512)(128)(4,1)S(1)}, pred[8]{0:T(512)(128)(4,1)}, u32[]{:S(2)}) copy-start(pred[8]{0:T(512)(128)(4,1)} %get-tuple-element.12) | copy-start | bytes 28
  139.1 90.0 %copy-start.6 = (f32[128]{0:T(128)S(1)}, f32[128]{0:T(128)}, u32[]{:S(2)}) copy-start(f32[128]{0:T(128)} %param.11) | copy-start | bytes 1540
  139.1 90.0 %copy-start.7 = (f32[128]{0:T(128)S(1)}, f32[128]{0:T(128)}, u32[]{:S(2)}) copy-start(f32[128]{0:T(128)} %param.10) | copy-start | bytes 1540
  140.7 88.4 %copy-start = (bf16[8,128,512]{2,1,0:T(8,128)(2,1)S(1)}, bf16[8,128,512]{2,1,0:T(8,128)(2,1)}, u32[]{:S(2)}) copy-start(bf16[8,128,512]{2,1,0:T(8,128)(2,1)} %gather_fusion.3) | copy-start | bytes 3145732
Sparse Core Ops, SparseCore 0:
  139.2 80.7 reduce-scatter.1
where the time goes:
time: 242 us; the launch traced here: 239 us
  waiting for transfers between devices  86.7 us (36%)
  local copies, waits for them, and re-layouts  75.9 us (31%)
  matrix products  39.2 us (16%)
  between operations  15.2 us (6%)
  starting transfers between devices  11.6 us (5%)
  other arithmetic  10.1 us (4%)
    reduce_scatter x1, waiting for transfers between devices, shards(): lax.psum_scatter(summed, 'chan', scatter_dimension=0, tiled=True)  79.2 us
    dot_general x3, matrix products, shards(): jnp.dot(weight_rows, stacks[offset], preferred_element_type=jnp.float32)  39.2 us
    another operation x6, local copies, waits for them, and re-layouts, columns(): return jnp.stack(pieces).reshape(9 * channels, frame_count * H * W)  35.6 us
    unnamed x55, local copies, waits for them, and re-layouts  20.4 us
    ppermute x1, starting transfers between devices, padded_2(): lax.ppermute(lax.slice_in_dim(block, 0, width, axis=dim), axis, backward)  8.21 us
    ppermute x1, waiting for transfers between devices, padded_2(): lax.ppermute(lax.slice_in_dim(block, block.shape[dim] - width, None, axis...  7.42 us
    select_n x3, local copies, waits for them, and re-layouts, columns(): jnp.take(extended, local_index, axis=1).reshape(channels, frame_count, H, W)  5.01 us
  transfers between devices with their start and end apart: 3, of which 2 were waited for; matrix products, arithmetic and copies ran while one was open for 7% of the time, Pallas kernels for 0%

commit v1 on v0

v1 whole, which is shorter than its diff:
```python
import jax
import jax.numpy as jnp
from jax import lax
from jax.experimental import pallas as pl
from jax.experimental.pallas import tpu as pltpu
from jax.sharding import PartitionSpec as P

MESH = pl.DeviceIdType.MESH
F32 = jnp.float32
BF16 = jnp.bfloat16

GROUPS = 32
NCLIP = 12
FRAMES = 4
CAP = 8
CELLS = 512
ROW = 32
OWN = 128
PAIR = 256
TAPS = 27

N_Y = 3
N_X = 2
Y0 = 0
X0 = Y0 + 4 * N_Y
D0 = X0 + 4 * N_X
N_ZIN = 3
N_ZOUT = TAPS - D0 - N_ZIN
norm_eps = 1e-06


def tap_at(pos):
    return lax.rem(pos, 3) * 9 + lax.div(pos, 3)


def conv_part(w_ref, frames):
    lane = lax.broadcasted_iota(jnp.int32, (1, CELLS), 1)
    column = lax.rem(lane, ROW)
    total = None
    for a in range(3):
        rows = None
        for b in range(3):
            part = None
            for k in range(3):
                term = jnp.dot(w_ref[9 * k + 3 * a + b], frames[k], preferred_element_type=F32)
                part = term if part is None else part + term
            if b == 0:
                part = jnp.where(column > 0, pltpu.roll(part, 1, axis=1), 0.0)
            if b == 2:
                part = jnp.where(column < ROW - 1, pltpu.roll(part, CELLS - 1, axis=1), 0.0)
            rows = part if rows is None else rows + part
        if a == 0:
            rows = jnp.where(lane >= ROW, pltpu.roll(rows, ROW, axis=1), 0.0)
        if a == 2:
            rows = jnp.where(lane < CELLS - ROW, pltpu.roll(rows, CELLS - ROW, axis=1), 0.0)
        total = rows if total is None else total + rows
    return total


def norm_block(summed, residual, gain, bias):
    width = 512 // GROUPS
    grouped = summed.reshape(OWN // width, width, CELLS)
    scale = 1.0 / (width * CELLS)
    average = jnp.sum(jnp.sum(grouped, axis=1, keepdims=True), axis=2, keepdims=True) * scale
    centred = grouped - average
    variance = jnp.sum(jnp.sum(centred * centred, axis=1, keepdims=True), axis=2, keepdims=True) * scale
    normed = (centred * lax.rsqrt(variance + norm_eps)).reshape(OWN, CELLS) * gain + bias
    return (normed / (1.0 + jnp.exp(-normed)) + residual.astype(F32)).astype(BF16)


def kernel(
    clips, bounds, x_ref, w_ref, gain_ref, bias_ref, out_ref,
    xn, xf, wn, wf, acc, blocks, column_pair,
    local_sem, sib_s, sib_r, zx_s, zx_r, fwd_s, fwd_r, halo_s, halo_r, hfwd_s, hfwd_r,
    zw_s, zw_r, xw_s, xw_r, yw_s, yw_r, blk_s, blk_r,
):
    t, c = lax.axis_index("tm"), lax.axis_index("chan")
    p, core = lax.div(c, 2), lax.rem(c, 2)
    y, zh, x = lax.div(t, 16), lax.rem(lax.div(t, 4), 4), lax.rem(t, 4)
    core_else, p_else = 1 - core, 1 - p
    c_sib, c_far, c_cross = 2 * p + core_else, 2 * p_else + core, 2 * p_else + core_else
    zh_out = lax.rem(zh + 3 + 2 * p, 4)
    t_out = (y * 4 + zh_out) * 4 + x

    def along_x(step):
        return (y * 4 + zh) * 4 + lax.rem(x + step, 4)

    def along_y(step):
        return (lax.rem(y + step, 4) * 4 + zh) * 4 + x

    t_next, t_prev = lax.rem(t + 1, 64), lax.rem(t + 63, 64)
    mine = pl.ds(pl.multiple_of(core * OWN, OWN), OWN)
    theirs = pl.ds(pl.multiple_of(core_else * OWN, OWN), OWN)

    barrier = pltpu.get_barrier_semaphore()
    partners = [(t, c_sib), (t, c_far), (t, c_cross), (t_out, c_far), (t_out, c_cross), (t_next, c), (t_prev, c)]
    partners += [(along_x(s), c) for s in (1, 2, 3)] + [(along_y(s), c) for s in (1, 2, 3)]
    for partner in partners:
        pl.semaphore_signal(barrier, inc=1, device_id=partner, device_id_type=MESH)

    def outputs_of(member):
        return pl.ds(pl.multiple_of(member * OWN, OWN), OWN)

    own_w = pltpu.make_async_copy(w_ref.at[:, outputs_of(c), :], wn.at[:, :, mine], local_sem)
    own_w.start()
    for f in range(FRAMES):
        xn[2 + f, mine, :] = x_ref[:, f, :]
    column_pair[0] = jnp.transpose(jnp.broadcast_to(gain_ref[...], (OWN, OWN)))
    column_pair[1] = jnp.transpose(jnp.broadcast_to(bias_ref[...], (OWN, OWN)))
    pl.semaphore_wait(barrier, len(partners))

    def send(src, dst, s, r, device):
        return pltpu.make_async_remote_copy(
            src_ref=src, dst_ref=dst, send_sem=s, recv_sem=r, device_id=device, device_id_type=MESH
        )

    started = []

    def go(copy):
        copy.start()
        started.append(copy)

    order = (2, 3, 0, 1)
    cross = {f: send(xn.at[2 + f, mine], xf.at[2 + f, mine], zx_s.at[f], zx_r.at[f], (t, c_far)) for f in order}
    for f in order:
        go(cross[f])
    sib_x = send(xn.at[pl.ds(2, FRAMES), mine], xn.at[pl.ds(2, FRAMES), mine], sib_s.at[0], sib_r.at[0], (t, c_sib))
    sib_w = send(w_ref.at[:, outputs_of(c_sib), :], wn.at[:, :, mine], sib_s.at[1], sib_r.at[1], (t, c_sib))
    go(sib_x)
    go(sib_w)
    slots = [("y", i) for i in range(N_Y)] + [("x", i) for i in range(N_X)]
    slots += [("d", D0 + i) for i in range(N_ZOUT)] + [("e", D0 + N_ZOUT + i) for i in range(N_ZIN)]

    def place(slot, sx, sy):
        kind, i = slot
        if kind == "y":
            return tap_at(Y0 + N_Y * sy + i)
        if kind == "x":
            return tap_at(X0 + N_X * sx + i)
        return (i % 3) * 9 + i // 3

    fetched = []
    for n, slot in enumerate(slots):
        tap = place(slot, x, y)
        t_to = t if slot[0] == "e" else t_out
        pair = []
        for role, member in enumerate((c_far, c_cross)):
            pair.append(
                send(
                    w_ref.at[tap, outputs_of(member), :], wf.at[tap, :, mine],
                    zw_s.at[n, role], zw_r.at[n, role], (t_to, member),
                )
            )
            go(pair[-1])
        fetched.append(pair)
    for h in range(2):
        go(send(xn.at[4 + h, mine], xn.at[h, mine], halo_s.at[h], halo_r.at[h], (t_next, c)))

    def arrived(src, dst, r):
        pltpu.make_async_remote_copy(
            src_ref=src, dst_ref=dst, send_sem=r, recv_sem=r, device_id=(t, c), device_id_type=MESH
        ).wait_recv()

    def await_weights(n):
        tap = place(slots[n], x, y)
        for role, lanes in enumerate((mine, theirs)):
            arrived(wf.at[tap, :, lanes], wf.at[tap, :, lanes], zw_r.at[n, role])

    def hand_on(n):
        await_weights(n)
        kind, i = slots[n]
        tap = place(slots[n], x, y)
        s, r, to = (yw_s, yw_r, along_y) if kind == "y" else (xw_s, xw_r, along_x)
        for step in (1, 2, 3):
            go(send(wf.at[tap], wf.at[tap], s.at[i, step - 1], r.at[i, step - 1], (to(step), c)))

    def pass_latents(f):
        arrived(xf.at[2 + f, mine], xf.at[2 + f, mine], zx_r.at[f])
        go(send(xf.at[2 + f, mine], xf.at[2 + f, mine], fwd_s.at[f], fwd_r.at[f], (t, c_sib)))
        if f >= 2:
            go(send(xf.at[2 + f, mine], xf.at[f - 2, mine], halo_s.at[f], halo_r.at[f], (t_next, c)))

    def pass_halo(n):
        buffer = xn if n < 2 else xf
        h = n % 2
        arrived(buffer.at[h, mine], buffer.at[h, mine], halo_r.at[n])
        go(send(buffer.at[h, mine], buffer.at[h, mine], hfwd_s.at[n], hfwd_r.at[n], (t, c_sib)))

    def await_halo(n):
        buffer = xn if n < 2 else xf
        h = n % 2
        arrived(buffer.at[h, theirs], buffer.at[h, theirs], hfwd_r.at[n])

    def sources(buffer, f):
        frame = t * FRAMES + f
        first, end = jnp.int32(0), jnp.int32(0)
        for n in range(NCLIP):
            first = jnp.where(end <= frame, end, first)
            end = end + clips[n]
        own = buffer[f + 2]
        before = jnp.where(first <= frame - 1, buffer[f + 1], own)
        earlier = jnp.where(first <= frame - 2, buffer[f], before)
        return earlier, before, own

    def near(f):
        acc[f] = conv_part(wn, sources(xn, f))

    own_w.wait()
    arrived(xn.at[pl.ds(2, FRAMES), theirs], xn.at[pl.ds(2, FRAMES), theirs], sib_r.at[0])
    arrived(wn.at[:, :, theirs], wn.at[:, :, theirs], sib_r.at[1])

    near(3)
    hand_on(0)
    pass_latents(2)
    near(2)
    hand_on(1)
    pass_halo(0)
    pass_halo(1)
    hand_on(2)
    pass_latents(3)
    await_halo(0)
    await_halo(1)
    near(1)
    hand_on(3)
    hand_on(4)
    near(0)
    pass_latents(0)
    pass_halo(2)
    pass_halo(3)
    pass_latents(1)

    for f in order:
        arrived(xf.at[2 + f, theirs], xf.at[2 + f, theirs], fwd_r.at[f])
    await_halo(2)
    await_halo(3)
    for n in range(N_Y + N_X, len(slots)):
        await_weights(n)
    for kind, count, r in (("x", N_X, xw_r), ("y", N_Y, yw_r)):
        for i in range(count):
            for step in (1, 2, 3):
                tap = place((kind, i), lax.rem(x + 4 - step, 4), lax.rem(y + 4 - step, 4))
                arrived(wf.at[tap], wf.at[tap], r.at[i, step - 1])

    gain, bias = column_pair[0, :, 0:1], column_pair[1, :, 0:1]
    sent = {}
    for f in (1, 2, 0, 3):
        summed = acc[f] + conv_part(wf, sources(xf, f))
        blocks[2 + f] = norm_block(summed, xn[2 + f, mine, :], gain, bias)
        to, slot = (t_prev, 6 + f) if f < 2 else (t_next, f - 2)
        go(send(blocks.at[2 + f], blocks.at[slot], blk_s.at[f], blk_r.at[f], (to, c)))
    for f in range(FRAMES):
        slot = 6 + f if f < 2 else f - 2
        arrived(blocks.at[slot], blocks.at[slot], blk_r.at[f])

    first, size = bounds[0, 0], bounds[0, 1] - bounds[0, 0]
    offset = first - (t * FRAMES - 2)
    columns = []
    for j in range(CAP):
        value = blocks[jnp.clip(offset + j, 0, CAP - 1)]
        columns.append(jnp.where(j < size, value, jnp.zeros_like(value)).astype(F32))
    out_ref[...] = jnp.stack(columns, axis=1).astype(BF16)
    for copy in started:
        copy.wait_send()


def shards(latents, conv_weight, norm_gain, norm_bias, clip_lengths, slab_bounds):
    weights = jnp.transpose(conv_weight, (1, 2, 0, 3)).reshape(TAPS, 512, OWN)
    vmem, smem, dma = pltpu.VMEM, pltpu.SMEM, pltpu.SemaphoreType.DMA
    n_slots = N_Y + N_X + N_ZOUT + N_ZIN
    return pl.pallas_call(
        kernel,
        out_shape=jax.ShapeDtypeStruct((OWN, CAP, CELLS), BF16),
        in_specs=[
            pl.BlockSpec(memory_space=smem),
            pl.BlockSpec(memory_space=smem),
            pl.BlockSpec(memory_space=vmem),
            pl.BlockSpec(memory_space=pl.ANY),
            pl.BlockSpec(memory_space=vmem),
            pl.BlockSpec(memory_space=vmem),
        ],
        out_specs=pl.BlockSpec(memory_space=vmem),
        scratch_shapes=[
            vmem((6, PAIR, CELLS), BF16),
            vmem((6, PAIR, CELLS), BF16),
            vmem((TAPS, OWN, PAIR), BF16),
            vmem((TAPS, OWN, PAIR), BF16),
            vmem((FRAMES, OWN, CELLS), F32),
            vmem((CAP, OWN, CELLS), BF16),
            vmem((2, OWN, OWN), F32),
            dma,
            dma((2,)), dma((2,)),
            dma((4,)), dma((4,)),
            dma((4,)), dma((4,)),
            dma((4,)), dma((4,)),
            dma((4,)), dma((4,)),
            dma((n_slots, 2)), dma((n_slots, 2)),
            dma((N_X, 3)), dma((N_X, 3)),
            dma((N_Y, 3)), dma((N_Y, 3)),
            dma((4,)), dma((4,)),
        ],
        compiler_params=pltpu.CompilerParams(
            collective_id=0, has_side_effects=True, vmem_limit_bytes=56 * 2**20
        ),
    )(clip_lengths, slab_bounds, latents, weights, norm_gain.reshape(1, OWN), norm_bias.reshape(1, OWN))


def solution(mesh):
    placed = (P("chan", "tm", None), P(None, None, None, "chan"), P("chan"), P("chan"), P(), P("tm", None))
    return jax.shard_map(
        shards, mesh=mesh, in_specs=placed, out_specs=P("chan", "tm", None), check_vma=False
    )
```

time: 242 us -> 74 us (0.31)
  the two profiles are of different devices: /device:TPU:56 before, /device:TPU:1 now
where the time goes in v1:
time: 74 us; the launch traced here: 73.8 us
  Pallas kernels  71.6 us (97%)
  local copies, waits for them, and re-layouts  2.26 us (3%)
    pallas_call x1, Pallas kernels, shards(): pl.pallas_call(kernel, out_shape=jax.ShapeDtypeStruct((OWN, CAP, CELLS),...  71.6 us
    unnamed x1, local copies, waits for them, and re-layouts  2.26 us

profile of v1, /device:TPU:1, one launch (start us, length us, event | category | flops | bytes accessed | tf_op | source)
XLA Modules:
  0.0 73.8 jit_solution(385786611768709476)
XLA Ops:
  0.0 71.6 %shard_map.64 = bf16[128,8,512]{2,1,0:T(8,128)(2,1)} custom-call(s32[12]{0:T(128)} %clips.1, s32[1,2]{1,0:T(1,128)} %bounds.1, bf16[128,4,512]{2,1,0:T(4,128)(2,1)} %x_ref.1, bf16[27,512,128]{2,1,0:T(8,128)(2,1)} %bitcast.5, f32[1,128]{1,0:T(1,128)} %bitcast.6, f32[1,128]{1,0:T(1,128)} %bitcast.7), custom_call_target="tpu_custom_call" | custom-call | tf_op jit(solution)/shard_map/pallas_call | solution.py:270
  71.6 2.3 %copy.8 = bf16[128,8,512]{2,1,0:T(8,128)(2,1)} copy(bf16[128,8,512]{2,1,0:T(8,128)(2,1)} %shard_map.64) | data formatting | bytes 2097152

commit v2 on v1

v2 whole, which is shorter than its diff:
```python
import jax
import jax.numpy as jnp
from jax import lax
from jax.experimental import pallas as pl
from jax.experimental.pallas import tpu as pltpu
from jax.sharding import PartitionSpec as P

MESH = pl.DeviceIdType.MESH
F32 = jnp.float32
BF16 = jnp.bfloat16

GROUPS = 32
NCLIP = 12
SLABS = 64
FRAMES = 4
CAP = 8
CELLS = 512
ROW = 32
OWN = 128
PAIR = 256
TAPS = 27
WIDTH = 512 // GROUPS
norm_eps = 1e-06


def conv_part(w_ref, side, frames):
    lane = lax.broadcasted_iota(jnp.int32, (1, CELLS), 1)
    column = lax.rem(lane, ROW)
    total = None
    for a in range(3):
        rows = None
        for b in range(3):
            part = None
            for k in range(3):
                tap = 9 * k + 3 * a + b
                weights = jnp.concatenate([w_ref[side, tap, 0], w_ref[side, tap, 1]], axis=1)
                term = jnp.dot(weights, frames[k], preferred_element_type=F32)
                part = term if part is None else part + term
            if b == 0:
                part = jnp.where(column > 0, pltpu.roll(part, 1, axis=1), 0.0)
            if b == 2:
                part = jnp.where(column < ROW - 1, pltpu.roll(part, CELLS - 1, axis=1), 0.0)
            rows = part if rows is None else rows + part
        if a == 0:
            rows = jnp.where(lane >= ROW, pltpu.roll(rows, ROW, axis=1), 0.0)
        if a == 2:
            rows = jnp.where(lane < CELLS - ROW, pltpu.roll(rows, CELLS - ROW, axis=1), 0.0)
        total = rows if total is None else total + rows
    return total


def norm_block(summed, residual, gain, bias):
    grouped = summed.reshape(OWN // WIDTH, WIDTH, CELLS)
    scale = 1.0 / (WIDTH * CELLS)
    average = jnp.sum(jnp.sum(grouped, axis=1, keepdims=True), axis=2, keepdims=True) * scale
    centred = grouped - average
    variance = jnp.sum(jnp.sum(centred * centred, axis=1, keepdims=True), axis=2, keepdims=True) * scale
    normed = (centred * lax.rsqrt(variance + norm_eps)).reshape(OWN, CELLS) * gain + bias
    return (normed / (1.0 + jnp.exp(-normed)) + residual.astype(F32)).astype(BF16)


def coded(summed):
    grouped = summed.reshape(OWN // WIDTH, WIDTH, CELLS)
    top = jnp.max(jnp.max(jnp.abs(grouped), axis=1, keepdims=True), axis=2, keepdims=True)
    step = jnp.maximum(top, 1e-30) * (1.0 / 32767.0)
    levels = jnp.round(grouped * (1.0 / step)).reshape(OWN, CELLS)
    return levels.astype(jnp.int32).astype(jnp.int16), jnp.broadcast_to(step.reshape(OWN // WIDTH, 1), (OWN // WIDTH, OWN))


def decoded(levels, steps):
    grouped = levels.astype(jnp.int32).astype(F32).reshape(OWN // WIDTH, WIDTH, CELLS)
    return (grouped * steps[:, 0:1].reshape(OWN // WIDTH, 1, 1)).reshape(OWN, CELLS)


def kernel(
    clips, bounds, x_ref, w_ref, gain_ref, bias_ref, out_ref,
    xn, weights, acc, q_out, q_in, step_out, step_in, blocks, column_pair,
    local_sem, sib_s, sib_r, halo_s, halo_r, hfwd_s, hfwd_r, q_s, q_r, step_s, step_r, blk_s, blk_r,
):
    t, c = lax.axis_index("tm"), lax.axis_index("chan")
    p, core = lax.div(c, 2), lax.rem(c, 2)
    core_else = 1 - core
    c_sib, c_far, c_cross = 2 * p + core_else, 2 * (1 - p) + core, 2 * (1 - p) + core_else
    t_next, t_prev = lax.rem(t + 1, SLABS), lax.rem(t + SLABS - 1, SLABS)
    has_next, has_prev = t < SLABS - 1, t > 0
    mine = pl.ds(pl.multiple_of(core * OWN, OWN), OWN)
    theirs = pl.ds(pl.multiple_of(core_else * OWN, OWN), OWN)

    barrier = pltpu.get_barrier_semaphore()

    def greet(partner):
        pl.semaphore_signal(barrier, inc=1, device_id=partner, device_id_type=MESH)

    greet((t, c_sib))
    greet((t, c_far))
    pl.when(has_next)(lambda: greet((t_next, c)))
    pl.when(has_prev)(lambda: greet((t_prev, c)))

    def outputs_of(member):
        return pl.ds(pl.multiple_of(member * OWN, OWN), OWN)

    own_w = [
        pltpu.make_async_copy(w_ref.at[:, outputs_of(member), :], weights.at[side, :, core], local_sem.at[side])
        for side, member in enumerate((c_far, c))
    ]
    for copy in own_w:
        copy.start()
    for f in range(FRAMES):
        xn[2 + f, mine, :] = x_ref[:, f, :]
    column_pair[0] = jnp.transpose(jnp.broadcast_to(gain_ref[...], (OWN, OWN)))
    column_pair[1] = jnp.transpose(jnp.broadcast_to(bias_ref[...], (OWN, OWN)))
    pl.semaphore_wait(barrier, 2 + has_next.astype(jnp.int32) + has_prev.astype(jnp.int32))

    def send(src, dst, s, r, device):
        return pltpu.make_async_remote_copy(
            src_ref=src, dst_ref=dst, send_sem=s, recv_sem=r, device_id=device, device_id_type=MESH
        )

    started = []

    def go(copy, when=None):
        if when is None:
            copy.start()
        else:
            pl.when(when)(copy.start)
        started.append((copy, when))

    go(send(xn.at[pl.ds(2, FRAMES), mine], xn.at[pl.ds(2, FRAMES), mine], sib_s.at[2], sib_r.at[2], (t, c_sib)))
    for side, member in enumerate((c_cross, c_sib)):
        go(send(w_ref.at[:, outputs_of(member), :], weights.at[side, :, core], sib_s.at[side], sib_r.at[side], (t, c_sib)))
    for h in (1, 0):
        go(send(xn.at[4 + h, mine], xn.at[h, mine], halo_s.at[h], halo_r.at[h], (t_next, c)), has_next)

    def arrived(dst, r, when=None):
        copy = pltpu.make_async_remote_copy(
            src_ref=dst, dst_ref=dst, send_sem=r, recv_sem=r, device_id=(t, c), device_id_type=MESH
        )
        if when is None:
            copy.wait_recv()
        else:
            pl.when(when)(copy.wait_recv)

    def pass_halo(h):
        arrived(xn.at[h, mine], halo_r.at[h], has_prev)
        go(send(xn.at[h, mine], xn.at[h, mine], hfwd_s.at[h], hfwd_r.at[h], (t, c_sib)), has_prev)

    def sources(f):
        frame = t * FRAMES + f
        first, end = jnp.int32(0), jnp.int32(0)
        for n in range(NCLIP):
            first = jnp.where(end <= frame, end, first)
            end = end + clips[n]
        own = xn[f + 2]
        before = jnp.where(first <= frame - 1, xn[f + 1], own)
        earlier = jnp.where(first <= frame - 2, xn[f], before)
        return earlier, before, own

    def theirs_of(f):
        levels, steps = coded(conv_part(weights, 0, sources(f)))
        q_out[f] = levels
        step_out[f] = steps
        go(send(q_out.at[f], q_in.at[f], q_s.at[f], q_r.at[f], (t, c_far)))
        go(send(step_out.at[f], step_in.at[f], step_s.at[f], step_r.at[f], (t, c_far)))

    def own_of(f):
        acc[f] = conv_part(weights, 1, sources(f))

    def finish(f):
        arrived(q_in.at[f], q_r.at[f])
        arrived(step_in.at[f], step_r.at[f])
        summed = acc[f] + decoded(q_in[f], step_in[f])
        gain, bias = column_pair[0, :, 0:1], column_pair[1, :, 0:1]
        blocks[2 + f] = norm_block(summed, xn[2 + f, mine, :], gain, bias)
        to, slot, when = (t_prev, 6 + f, has_prev) if f < 2 else (t_next, f - 2, has_next)
        go(send(blocks.at[2 + f], blocks.at[slot], blk_s.at[f], blk_r.at[f], (to, c)), when)

    @pl.when(jnp.logical_not(has_prev))
    def _():
        for h in range(2):
            xn[h] = jnp.zeros((PAIR, CELLS), BF16)
            blocks[h] = jnp.zeros((OWN, CELLS), BF16)

    @pl.when(jnp.logical_not(has_next))
    def _():
        for h in range(2):
            blocks[6 + h] = jnp.zeros((OWN, CELLS), BF16)

    own_w[0].wait()
    arrived(xn.at[pl.ds(2, FRAMES), theirs], sib_r.at[2])
    arrived(weights.at[0, :, core_else], sib_r.at[0])
    theirs_of(3)
    theirs_of(2)
    own_w[1].wait()
    arrived(weights.at[1, :, core_else], sib_r.at[1])
    own_of(3)
    pass_halo(1)
    own_of(2)
    pass_halo(0)
    arrived(xn.at[1, theirs], hfwd_r.at[1], has_prev)
    theirs_of(1)
    arrived(xn.at[0, theirs], hfwd_r.at[0], has_prev)
    theirs_of(0)
    finish(3)
    finish(2)
    own_of(1)
    own_of(0)
    finish(1)
    finish(0)

    for f in range(FRAMES):
        slot, when = (6 + f, has_next) if f < 2 else (f - 2, has_prev)
        arrived(blocks.at[slot], blk_r.at[f], when)

    first, size = bounds[0, 0], bounds[0, 1] - bounds[0, 0]
    offset = first - (t * FRAMES - 2)
    columns = []
    for j in range(CAP):
        value = blocks[jnp.clip(offset + j, 0, CAP - 1)]
        columns.append(jnp.where(j < size, value, jnp.zeros_like(value)).astype(F32))
    out_ref[...] = jnp.stack(columns, axis=1).astype(BF16)
    for copy, when in started:
        if when is None:
            copy.wait_send()
        else:
            pl.when(when)(copy.wait_send)


def shards(latents, conv_weight, norm_gain, norm_bias, clip_lengths, slab_bounds):
    weights = jnp.transpose(conv_weight, (1, 2, 0, 3)).reshape(TAPS, 512, OWN)
    vmem, smem, dma = pltpu.VMEM, pltpu.SMEM, pltpu.SemaphoreType.DMA
    return pl.pallas_call(
        kernel,
        out_shape=jax.ShapeDtypeStruct((OWN, CAP, CELLS), BF16),
        in_specs=[
            pl.BlockSpec(memory_space=smem),
            pl.BlockSpec(memory_space=smem),
            pl.BlockSpec(memory_space=vmem),
            pl.BlockSpec(memory_space=pl.ANY),
            pl.BlockSpec(memory_space=vmem),
            pl.BlockSpec(memory_space=vmem),
        ],
        out_specs=pl.BlockSpec(memory_space=vmem),
        scratch_shapes=[
            vmem((6, PAIR, CELLS), BF16),
            vmem((2, TAPS, 2, OWN, OWN), BF16),
            vmem((FRAMES, OWN, CELLS), F32),
            vmem((FRAMES, OWN, CELLS), jnp.int16),
            vmem((FRAMES, OWN, CELLS), jnp.int16),
            vmem((FRAMES, OWN // WIDTH, OWN), F32),
            vmem((FRAMES, OWN // WIDTH, OWN), F32),
            vmem((CAP, OWN, CELLS), BF16),
            vmem((2, OWN, OWN), F32),
            dma((2,)),
            dma((3,)), dma((3,)),
            dma((2,)), dma((2,)),
            dma((2,)), dma((2,)),
            dma((4,)), dma((4,)),
            dma((4,)), dma((4,)),
            dma((4,)), dma((4,)),
        ],
        compiler_params=pltpu.CompilerParams(
            collective_id=0, has_side_effects=True, vmem_limit_bytes=56 * 2**20
        ),
    )(clip_lengths, slab_bounds, latents, weights, norm_gain.reshape(1, OWN), norm_bias.reshape(1, OWN))


def solution(mesh):
    placed = (P("chan", "tm", None), P(None, None, None, "chan"), P("chan"), P("chan"), P(), P("tm", None))
    return jax.shard_map(
        shards, mesh=mesh, in_specs=placed, out_specs=P("chan", "tm", None), check_vma=False
    )
```

time: 74 us -> 51 us (0.69)
  the two profiles are of different devices: /device:TPU:1 before, /device:TPU:94 now
where the time goes in v2:
time: 51 us; the launch traced here: 50.9 us
  Pallas kernels  48.6 us (95%)
  local copies, waits for them, and re-layouts  2.26 us (4%)
    pallas_call x1, Pallas kernels, shards(): pl.pallas_call(kernel, out_shape=jax.ShapeDtypeStruct((OWN, CAP, CELLS),...  48.6 us
    unnamed x1, local copies, waits for them, and re-layouts  2.26 us

profile of v2, /device:TPU:94, one launch (start us, length us, event | category | flops | bytes accessed | tf_op | source)
XLA Modules:
  0.0 50.9 jit_solution(13642399294929014234)
XLA Ops:
  0.0 48.6 %shard_map.64 = bf16[128,8,512]{2,1,0:T(8,128)(2,1)} custom-call(s32[12]{0:T(128)} %clips.1, s32[1,2]{1,0:T(1,128)} %bounds.1, bf16[128,4,512]{2,1,0:T(4,128)(2,1)} %x_ref.1, bf16[27,512,128]{2,1,0:T(8,128)(2,1)} %bitcast.5, f32[1,128]{1,0:T(1,128)} %bitcast.6, f32[1,128]{1,0:T(1,128)} %bitcast.7), custom_call_target="tpu_custom_call" | custom-call | tf_op jit(solution)/shard_map/pallas_call | solution.py:231
  48.6 2.3 %copy.8 = bf16[128,8,512]{2,1,0:T(8,128)(2,1)} copy(bf16[128,8,512]{2,1,0:T(8,128)(2,1)} %shard_map.64) | data formatting | bytes 2097152

commit v3 on v2

--- a/solution.py
+++ b/solution.py
@@ -12,6 +12,8 @@
 GROUPS = 32
 NCLIP = 12
 SLABS = 64
+RING = 4
+MOST = 6
 FRAMES = 4
 CAP = 8
 CELLS = 512
@@ -74,8 +76,8 @@
 
 def kernel(
     clips, bounds, x_ref, w_ref, gain_ref, bias_ref, out_ref,
-    xn, weights, acc, q_out, q_in, step_out, step_in, blocks, column_pair,
-    local_sem, sib_s, sib_r, halo_s, halo_r, hfwd_s, hfwd_r, q_s, q_r, step_s, step_r, blk_s, blk_r,
+    xn, weights, acc, q_out, q_in, step_out, step_in, blocks, column_pair, relay,
+    local_sem, sib_s, sib_r, halo_s, halo_r, hfwd_s, hfwd_r, q_s, q_r, step_s, step_r, blk_s, blk_r, relay_s, relay_r, ext_s, ext_r, efwd_s, efwd_r,
 ):
     t, c = lax.axis_index("tm"), lax.axis_index("chan")
     p, core = lax.div(c, 2), lax.rem(c, 2)
@@ -83,6 +85,15 @@
     c_sib, c_far, c_cross = 2 * p + core_else, 2 * (1 - p) + core, 2 * (1 - p) + core_else
     t_next, t_prev = lax.rem(t + 1, SLABS), lax.rem(t + SLABS - 1, SLABS)
     has_next, has_prev = t < SLABS - 1, t > 0
+    x = lax.rem(t, RING)
+    at_low, at_high = x == 0, x == RING - 1
+    not_low, not_high = x > 0, x < RING - 1
+    ring_next, ring_prev = t < SLABS - RING, t >= RING
+
+    def slab(step):
+        return lax.rem(t + SLABS + step, SLABS)
+
+    extra = at_high & has_next
     mine = pl.ds(pl.multiple_of(core * OWN, OWN), OWN)
     theirs = pl.ds(pl.multiple_of(core_else * OWN, OWN), OWN)
 
@@ -91,10 +102,13 @@
     def greet(partner):
         pl.semaphore_signal(barrier, inc=1, device_id=partner, device_id_type=MESH)
 
+    partners = [(has_next, 1), (has_prev, -1), (at_high, -2), (at_high, -3)]
+    partners += [((x == 2) & ring_next, 2), (x == 1, 2), ((x == 1) & ring_next, 3)]
+    partners += [(at_low, 3), (at_low & ring_next, 4)] + [(at_low & ring_prev, -step) for step in (2, 3, 4)]
     greet((t, c_sib))
     greet((t, c_far))
-    pl.when(has_next)(lambda: greet((t_next, c)))
-    pl.when(has_prev)(lambda: greet((t_prev, c)))
+    for when, step in partners:
+        pl.when(when)(lambda step=step: greet((slab(step), c)))
 
     def outputs_of(member):
         return pl.ds(pl.multiple_of(member * OWN, OWN), OWN)
@@ -109,7 +123,7 @@
         xn[2 + f, mine, :] = x_ref[:, f, :]
     column_pair[0] = jnp.transpose(jnp.broadcast_to(gain_ref[...], (OWN, OWN)))
     column_pair[1] = jnp.transpose(jnp.broadcast_to(bias_ref[...], (OWN, OWN)))
-    pl.semaphore_wait(barrier, 2 + has_next.astype(jnp.int32) + has_prev.astype(jnp.int32))
+    pl.semaphore_wait(barrier, 2 + sum(when.astype(jnp.int32) for when, _ in partners))
 
     def send(src, dst, s, r, device):
         return pltpu.make_async_remote_copy(
@@ -118,18 +132,23 @@
 
     started = []
 
-    def go(copy, when=None):
+    def go(copy, when=None, keep=True):
         if when is None:
             copy.start()
         else:
             pl.when(when)(copy.start)
-        started.append((copy, when))
+        if keep:
+            started.append((copy, when))
 
     go(send(xn.at[pl.ds(2, FRAMES), mine], xn.at[pl.ds(2, FRAMES), mine], sib_s.at[2], sib_r.at[2], (t, c_sib)))
     for side, member in enumerate((c_cross, c_sib)):
         go(send(w_ref.at[:, outputs_of(member), :], weights.at[side, :, core], sib_s.at[side], sib_r.at[side], (t, c_sib)))
-    for h in (1, 0):
-        go(send(xn.at[4 + h, mine], xn.at[h, mine], halo_s.at[h], halo_r.at[h], (t_next, c)), has_next)
+    go(send(xn.at[5, mine], xn.at[1, mine], halo_s.at[1], halo_r.at[1], (t_next, c)), has_next)
+    go(send(xn.at[4, mine], xn.at[0, mine], halo_s.at[0], halo_r.at[0], (t_next, c)), has_next & not_high)
+    go(send(xn.at[4, mine], relay.at[0], halo_s.at[0], relay_r.at[0], (slab(-3), c)), has_next & at_high)
+
+    for h in range(2):
+        go(send(xn.at[2 + h, mine], xn.at[6 + h, mine], ext_s.at[h], ext_r.at[h], (t_prev, c)), has_prev & at_low)
 
     def arrived(dst, r, when=None):
         copy = pltpu.make_async_remote_copy(
@@ -140,9 +159,26 @@
         else:
             pl.when(when)(copy.wait_recv)
 
+    passed = [send(xn.at[h, mine], xn.at[h, mine], hfwd_s.at[h], hfwd_r.at[h], (t, c_sib)) for h in range(2)]
+    started += [(copy, has_prev) for copy in passed]
+
     def pass_halo(h):
-        arrived(xn.at[h, mine], halo_r.at[h], has_prev)
-        go(send(xn.at[h, mine], xn.at[h, mine], hfwd_s.at[h], hfwd_r.at[h], (t, c_sib)), has_prev)
+        arrived(xn.at[h, mine], halo_r.at[h])
+        passed[h].start()
+        arrived(xn.at[h, theirs], hfwd_r.at[h])
+
+    def relay_on(n, place, dst, r, step):
+        when = (x == place) & ring_next
+        arrived(relay.at[n], relay_r.at[n], when)
+        go(send(relay.at[n], dst, relay_s.at[n], r, (slab(step), c)), when)
+
+    extra_passed = [send(xn.at[6 + h, mine], xn.at[6 + h, mine], efwd_s.at[h], efwd_r.at[h], (t, c_sib)) for h in range(2)]
+    started += [(copy, extra) for copy in extra_passed]
+
+    def pass_extra(h):
+        arrived(xn.at[6 + h, mine], ext_r.at[h])
+        extra_passed[h].start()
+        arrived(xn.at[6 + h, theirs], efwd_r.at[h])
 
     def sources(f):
         frame = t * FRAMES + f
@@ -155,24 +191,31 @@
         earlier = jnp.where(first <= frame - 2, xn[f], before)
         return earlier, before, own
 
-    def theirs_of(f):
+    def theirs_of(f, keep=True):
         levels, steps = coded(conv_part(weights, 0, sources(f)))
         q_out[f] = levels
         step_out[f] = steps
-        go(send(q_out.at[f], q_in.at[f], q_s.at[f], q_r.at[f], (t, c_far)))
-        go(send(step_out.at[f], step_in.at[f], step_s.at[f], step_r.at[f], (t, c_far)))
+        go(send(q_out.at[f], q_in.at[f], q_s.at[f], q_r.at[f], (t, c_far)), None, keep)
+        go(send(step_out.at[f], step_in.at[f], step_s.at[f], step_r.at[f], (t, c_far)), None, keep)
 
     def own_of(f):
         acc[f] = conv_part(weights, 1, sources(f))
 
-    def finish(f):
+    def merge(f):
         arrived(q_in.at[f], q_r.at[f])
         arrived(step_in.at[f], step_r.at[f])
         summed = acc[f] + decoded(q_in[f], step_in[f])
         gain, bias = column_pair[0, :, 0:1], column_pair[1, :, 0:1]
         blocks[2 + f] = norm_block(summed, xn[2 + f, mine, :], gain, bias)
-        to, slot, when = (t_prev, 6 + f, has_prev) if f < 2 else (t_next, f - 2, has_next)
-        go(send(blocks.at[2 + f], blocks.at[slot], blk_s.at[f], blk_r.at[f], (to, c)), when)
+
+    def finish(f):
+        merge(f)
+        if f < 2:
+            go(send(blocks.at[2 + f], blocks.at[6 + f], blk_s.at[f], blk_r.at[f], (t_prev, c)), has_prev & not_low)
+            return
+        go(send(blocks.at[2 + f], blocks.at[f - 2], blk_s.at[f], blk_r.at[f], (t_next, c)), has_next & not_high)
+        n, to = (1, slab(-1)) if f == 3 else (2, slab(-2))
+        go(send(blocks.at[2 + f], relay.at[n], blk_s.at[f], relay_r.at[n], (to, c)), has_next & at_high)
 
     @pl.when(jnp.logical_not(has_prev))
     def _():
@@ -193,22 +236,42 @@
     own_w[1].wait()
     arrived(weights.at[1, :, core_else], sib_r.at[1])
     own_of(3)
-    pass_halo(1)
+    pl.when(not_low)(lambda: pass_halo(1))
+    relay_on(0, 0, xn.at[0, mine], halo_r.at[0], 4)
     own_of(2)
-    pass_halo(0)
-    arrived(xn.at[1, theirs], hfwd_r.at[1], has_prev)
+    pl.when(at_low & has_prev)(lambda: pass_halo(1))
+    pl.when(not_low)(lambda: pass_halo(0))
     theirs_of(1)
-    arrived(xn.at[0, theirs], hfwd_r.at[0], has_prev)
-    theirs_of(0)
     finish(3)
+    pl.when(not_low)(lambda: theirs_of(0, False))
     finish(2)
     own_of(1)
+    pl.when(at_low & has_prev)(lambda: pass_halo(0))
+    pl.when(at_low)(lambda: theirs_of(0, False))
     own_of(0)
+    relay_on(1, 2, blocks.at[1], blk_r.at[3], 2)
+
+    @pl.when(extra)
+    def _():
+        pass_extra(0)
+        pass_extra(1)
+        lax.fori_loop(FRAMES, FRAMES + 2, lambda f, carry: (theirs_of(f, False), carry)[1], 0)
+
     finish(1)
+    relay_on(2, 1, blocks.at[0], blk_r.at[2], 3)
     finish(0)
 
+    @pl.when(extra)
+    def _():
+        def both(f, carry):
+            own_of(f)
+            merge(f)
+            return carry
+
+        lax.fori_loop(FRAMES, FRAMES + 2, both, 0)
+
     for f in range(FRAMES):
-        slot, when = (6 + f, has_next) if f < 2 else (f - 2, has_prev)
+        slot, when = (6 + f, has_next & not_high) if f < 2 else (f - 2, has_prev)
         arrived(blocks.at[slot], blk_r.at[f], when)
 
     first, size = bounds[0, 0], bounds[0, 1] - bounds[0, 0]
@@ -218,6 +281,9 @@
         value = blocks[jnp.clip(offset + j, 0, CAP - 1)]
         columns.append(jnp.where(j < size, value, jnp.zeros_like(value)).astype(F32))
     out_ref[...] = jnp.stack(columns, axis=1).astype(BF16)
+    for f, when in ((0, None), (4, extra), (5, extra)):
+        started.append((send(q_out.at[f], q_in.at[f], q_s.at[f], q_r.at[f], (t, c_far)), when))
+        started.append((send(step_out.at[f], step_in.at[f], step_s.at[f], step_r.at[f], (t, c_far)), when))
     for copy, when in started:
         if when is None:
             copy.wait_send()
@@ -241,22 +307,26 @@
         ],
         out_specs=pl.BlockSpec(memory_space=vmem),
         scratch_shapes=[
-            vmem((6, PAIR, CELLS), BF16),
+            vmem((CAP, PAIR, CELLS), BF16),
             vmem((2, TAPS, 2, OWN, OWN), BF16),
-            vmem((FRAMES, OWN, CELLS), F32),
-            vmem((FRAMES, OWN, CELLS), jnp.int16),
-            vmem((FRAMES, OWN, CELLS), jnp.int16),
-            vmem((FRAMES, OWN // WIDTH, OWN), F32),
-            vmem((FRAMES, OWN // WIDTH, OWN), F32),
+            vmem((MOST, OWN, CELLS), F32),
+            vmem((MOST, OWN, CELLS), jnp.int16),
+            vmem((MOST, OWN, CELLS), jnp.int16),
+            vmem((MOST, OWN // WIDTH, OWN), F32),
+            vmem((MOST, OWN // WIDTH, OWN), F32),
             vmem((CAP, OWN, CELLS), BF16),
             vmem((2, OWN, OWN), F32),
+            vmem((3, OWN, CELLS), BF16),
             dma((2,)),
             dma((3,)), dma((3,)),
             dma((2,)), dma((2,)),
             dma((2,)), dma((2,)),
+            dma((MOST,)), dma((MOST,)),
+            dma((MOST,)), dma((MOST,)),
             dma((4,)), dma((4,)),
-            dma((4,)), dma((4,)),
-            dma((4,)), dma((4,)),
+            dma((3,)), dma((3,)),
+            dma((2,)), dma((2,)),
+            dma((2,)), dma((2,)),
         ],
         compiler_params=pltpu.CompilerParams(
             collective_id=0, has_side_effects=True, vmem_limit_bytes=56 * 2**20

time: 51 us -> 42.5 us (0.83)
  the two profiles are of different devices: /device:TPU:94 before, /device:TPU:56 now
where the time goes in v3:
time: 42.5 us; the launch traced here: 41.9 us
  Pallas kernels  39.6 us (93%)
  local copies, waits for them, and re-layouts  2.26 us (5%)
    pallas_call x1, Pallas kernels, shards(): pl.pallas_call(kernel, out_shape=jax.ShapeDtypeStruct((OWN, CAP, CELLS),...  39.6 us
    unnamed x1, local copies, waits for them, and re-layouts  2.26 us

profile of v3, /device:TPU:56, one launch (start us, length us, event | category | flops | bytes accessed | tf_op | source)
XLA Modules:
  0.0 41.9 jit_solution(3105995240316331943)
XLA Ops:
  0.0 39.6 %shard_map.64 = bf16[128,8,512]{2,1,0:T(8,128)(2,1)} custom-call(s32[12]{0:T(128)} %clips.1, s32[1,2]{1,0:T(1,128)} %bounds.1, bf16[128,4,512]{2,1,0:T(4,128)(2,1)} %x_ref.1, bf16[27,512,128]{2,1,0:T(8,128)(2,1)} %bitcast.5, f32[1,128]{1,0:T(1,128)} %bitcast.6, f32[1,128]{1,0:T(1,128)} %bitcast.7), custom_call_target="tpu_custom_call" | custom-call | tf_op jit(solution)/shard_map/pallas_call | solution.py:297
  39.6 2.3 %copy.8 = bf16[128,8,512]{2,1,0:T(8,128)(2,1)} copy(bf16[128,8,512]{2,1,0:T(8,128)(2,1)} %shard_map.64) | data formatting | bytes 2097152

commit v4 on v3

--- a/solution.py
+++ b/solution.py
@@ -20,22 +20,24 @@
 ROW = 32
 OWN = 128
 PAIR = 256
-TAPS = 27
+HALF = 64
+PIECES = 4
 WIDTH = 512 // GROUPS
 norm_eps = 1e-06
 
 
-def conv_part(w_ref, side, frames):
+def conv_part(w_ref, side, frames, before_row=lambda a: None):
     lane = lax.broadcasted_iota(jnp.int32, (1, CELLS), 1)
     column = lax.rem(lane, ROW)
     total = None
     for a in range(3):
+        before_row(a)
         rows = None
         for b in range(3):
             part = None
             for k in range(3):
-                tap = 9 * k + 3 * a + b
-                weights = jnp.concatenate([w_ref[side, tap, 0], w_ref[side, tap, 1]], axis=1)
+                tap = 3 * a + b
+                weights = jnp.concatenate([w_ref[side, k, tap, 0], w_ref[side, k, tap, 1]], axis=1)
                 term = jnp.dot(weights, frames[k], preferred_element_type=F32)
                 part = term if part is None else part + term
             if b == 0:
@@ -75,9 +77,9 @@
 
 
 def kernel(
-    clips, bounds, x_ref, w_ref, gain_ref, bias_ref, out_ref,
-    xn, weights, acc, q_out, q_in, step_out, step_in, blocks, column_pair, relay,
-    local_sem, sib_s, sib_r, halo_s, halo_r, hfwd_s, hfwd_r, q_s, q_r, step_s, step_r, blk_s, blk_r, relay_s, relay_r, ext_s, ext_r, efwd_s, efwd_r,
+    clips, bounds, x_hbm, w_ref, gain_ref, bias_ref, out_ref,
+    x_ref, slots, xn, weights, acc, q_out, q_in, step_out, step_in, blocks, column_pair, relay, relay_blk,
+    local_sem, sib_s, sib_r, halo_s, halo_r, hfwd_s, hfwd_r, q_s, q_r, step_s, step_r, blk_s, blk_r, relay_s, relay_r, edge_s, edge_r, half_s, half_r, on_s, on_r, ext_s, ext_r, efwd_s, efwd_r,
 ):
     t, c = lax.axis_index("tm"), lax.axis_index("chan")
     p, core = lax.div(c, 2), lax.rem(c, 2)
@@ -113,16 +115,19 @@
     def outputs_of(member):
         return pl.ds(pl.multiple_of(member * OWN, OWN), OWN)
 
+    own_x = pltpu.make_async_copy(x_hbm, x_ref, local_sem.at[2])
+    own_x.start()
     own_w = [
-        pltpu.make_async_copy(w_ref.at[:, outputs_of(member), :], weights.at[side, :, core], local_sem.at[side])
+        pltpu.make_async_copy(w_ref.at[:, :, outputs_of(member), :], weights.at[side, :, :, core], local_sem.at[side])
         for side, member in enumerate((c_far, c))
     ]
     for copy in own_w:
         copy.start()
-    for f in range(FRAMES):
-        xn[2 + f, mine, :] = x_ref[:, f, :]
     column_pair[0] = jnp.transpose(jnp.broadcast_to(gain_ref[...], (OWN, OWN)))
     column_pair[1] = jnp.transpose(jnp.broadcast_to(bias_ref[...], (OWN, OWN)))
+    own_x.wait()
+    for f in (3, 2, 1):
+        xn[2 + f, mine, :] = x_ref[:, f, :]
     pl.semaphore_wait(barrier, 2 + sum(when.astype(jnp.int32) for when, _ in partners))
 
     def send(src, dst, s, r, device):
@@ -140,15 +145,28 @@
         if keep:
             started.append((copy, when))
 
-    go(send(xn.at[pl.ds(2, FRAMES), mine], xn.at[pl.ds(2, FRAMES), mine], sib_s.at[2], sib_r.at[2], (t, c_sib)))
-    for side, member in enumerate((c_cross, c_sib)):
-        go(send(w_ref.at[:, outputs_of(member), :], weights.at[side, :, core], sib_s.at[side], sib_r.at[side], (t, c_sib)))
+    def share_x(f):
+        go(send(xn.at[2 + f, mine], xn.at[2 + f, mine], sib_s.at[f], sib_r.at[f], (t, c_sib)))
+
+    def share_w(side, rows, n):
+        src = w_ref.at[:, rows, outputs_of((c_cross, c_sib)[side]), :]
+        go(send(src, weights.at[side, :, rows, core], sib_s.at[n], sib_r.at[n], (t, c_sib)))
+
+    for f in (3, 2, 1):
+        share_x(f)
+    for a in range(3):
+        share_w(0, pl.ds(3 * a, 3), 4 + a)
+    xn[2, mine, :] = x_ref[:, 0, :]
+    share_x(0)
     go(send(xn.at[5, mine], xn.at[1, mine], halo_s.at[1], halo_r.at[1], (t_next, c)), has_next)
     go(send(xn.at[4, mine], xn.at[0, mine], halo_s.at[0], halo_r.at[0], (t_next, c)), has_next & not_high)
-    go(send(xn.at[4, mine], relay.at[0], halo_s.at[0], relay_r.at[0], (slab(-3), c)), has_next & at_high)
-
+    halves = [pl.ds(pl.multiple_of(core * OWN + HALF * part, HALF), HALF) for part in range(2)]
+    for part in range(2):
+        go(send(xn.at[4, halves[part]], relay.at[part], edge_s.at[part], relay_r.at[part], (slab(-3), c)), has_next & at_high)
     for h in range(2):
         go(send(xn.at[2 + h, mine], xn.at[6 + h, mine], ext_s.at[h], ext_r.at[h], (t_prev, c)), has_prev & at_low)
+
+    share_w(1, pl.ds(0, 9), 7)
 
     def arrived(dst, r, when=None):
         copy = pltpu.make_async_remote_copy(
@@ -162,15 +180,28 @@
     passed = [send(xn.at[h, mine], xn.at[h, mine], hfwd_s.at[h], hfwd_r.at[h], (t, c_sib)) for h in range(2)]
     started += [(copy, has_prev) for copy in passed]
 
-    def pass_halo(h):
-        arrived(xn.at[h, mine], halo_r.at[h])
+    def pass_halo(h, relayed=False):
+        if relayed:
+            for part in range(2):
+                arrived(xn.at[h, halves[part]], edge_r.at[part])
+        else:
+            arrived(xn.at[h, mine], halo_r.at[h])
         passed[h].start()
+
+    def await_halo(h):
         arrived(xn.at[h, theirs], hfwd_r.at[h])
 
-    def relay_on(n, place, dst, r, step):
-        when = (x == place) & ring_next
-        arrived(relay.at[n], relay_r.at[n], when)
-        go(send(relay.at[n], dst, relay_s.at[n], r, (slab(step), c)), when)
+    def relay_halo():
+        for part in range(2):
+            arrived(relay.at[part], relay_r.at[part], at_low & ring_next)
+            dst = xn.at[0, halves[part]]
+            go(send(relay.at[part], dst, relay_s.at[part], edge_r.at[part], (slab(4), c)), at_low & ring_next)
+
+    def relay_block(f, part):
+        n, when = 2 * (3 - f) + part, (x == 2 - part) & ring_next
+        arrived(relay_blk.at[n], half_r.at[n], when)
+        dst = blocks.at[f - 2, pl.ds(HALF * part, HALF)]
+        go(send(relay_blk.at[n], dst, on_s.at[n], on_r.at[n], (slab(2 + part), c)), when)
 
     extra_passed = [send(xn.at[6 + h, mine], xn.at[6 + h, mine], efwd_s.at[h], efwd_r.at[h], (t, c_sib)) for h in range(2)]
     started += [(copy, extra) for copy in extra_passed]
@@ -178,6 +209,8 @@
     def pass_extra(h):
         arrived(xn.at[6 + h, mine], ext_r.at[h])
         extra_passed[h].start()
+
+    def await_extra(h):
         arrived(xn.at[6 + h, theirs], efwd_r.at[h])
 
     def sources(f):
@@ -191,8 +224,8 @@
         earlier = jnp.where(first <= frame - 2, xn[f], before)
         return earlier, before, own
 
-    def theirs_of(f, keep=True):
-        levels, steps = coded(conv_part(weights, 0, sources(f)))
+    def theirs_of(f, keep=True, before_row=lambda a: None):
+        levels, steps = coded(conv_part(weights, 0, sources(f), before_row))
         q_out[f] = levels
         step_out[f] = steps
         go(send(q_out.at[f], q_in.at[f], q_s.at[f], q_r.at[f], (t, c_far)), None, keep)
@@ -214,8 +247,10 @@
             go(send(blocks.at[2 + f], blocks.at[6 + f], blk_s.at[f], blk_r.at[f], (t_prev, c)), has_prev & not_low)
             return
         go(send(blocks.at[2 + f], blocks.at[f - 2], blk_s.at[f], blk_r.at[f], (t_next, c)), has_next & not_high)
-        n, to = (1, slab(-1)) if f == 3 else (2, slab(-2))
-        go(send(blocks.at[2 + f], relay.at[n], blk_s.at[f], relay_r.at[n], (to, c)), has_next & at_high)
+        for part in range(2):
+            n = 2 * (3 - f) + part
+            src = blocks.at[2 + f, pl.ds(HALF * part, HALF)]
+            go(send(src, relay_blk.at[n], half_s.at[n], half_r.at[n], (slab(-1 - part), c)), has_next & at_high)
 
     @pl.when(jnp.logical_not(has_prev))
     def _():
@@ -228,38 +263,66 @@
         for h in range(2):
             blocks[6 + h] = jnp.zeros((OWN, CELLS), BF16)
 
+    def await_row(a):
+        rows = pl.ds(3 * a, 3)
+        arrived(weights.at[0, :, rows, core_else], sib_r.at[4 + a])
+
     own_w[0].wait()
-    arrived(xn.at[pl.ds(2, FRAMES), theirs], sib_r.at[2])
-    arrived(weights.at[0, :, core_else], sib_r.at[0])
-    theirs_of(3)
+    for f in (3, 2, 1):
+        arrived(xn.at[2 + f, theirs], sib_r.at[f])
+    theirs_of(3, before_row=await_row)
+    arrived(xn.at[2, theirs], sib_r.at[0])
     theirs_of(2)
+    pl.when(not_low)(lambda: pass_halo(1))
     own_w[1].wait()
-    arrived(weights.at[1, :, core_else], sib_r.at[1])
+    arrived(weights.at[1, :, :, core_else], sib_r.at[7])
     own_of(3)
-    pl.when(not_low)(lambda: pass_halo(1))
-    relay_on(0, 0, xn.at[0, mine], halo_r.at[0], 4)
+    relay_halo()
+
+    @pl.when(not_low)
+    def _():
+        await_halo(1)
+        theirs_of(1, False)
+        pass_halo(0)
+
     own_of(2)
-    pl.when(at_low & has_prev)(lambda: pass_halo(1))
-    pl.when(not_low)(lambda: pass_halo(0))
-    theirs_of(1)
     finish(3)
-    pl.when(not_low)(lambda: theirs_of(0, False))
+    pl.when(extra)(lambda: pass_extra(0))
+
+    @pl.when(not_low)
+    def _():
+        await_halo(0)
+        theirs_of(0, False)
+
+    @pl.when(at_low)
+    def _():
+        pl.when(has_prev)(lambda: (pass_halo(1), await_halo(1))[0])
+        theirs_of(1, False)
+
+    own_of(1)
     finish(2)
-    own_of(1)
-    pl.when(at_low & has_prev)(lambda: pass_halo(0))
+    pl.when(at_low & has_prev)(lambda: (pass_halo(0, True), await_halo(0))[0])
     pl.when(at_low)(lambda: theirs_of(0, False))
     own_of(0)
-    relay_on(1, 2, blocks.at[1], blk_r.at[3], 2)
 
     @pl.when(extra)
     def _():
-        pass_extra(0)
+        await_extra(0)
+        theirs_of(4, False)
         pass_extra(1)
-        lax.fori_loop(FRAMES, FRAMES + 2, lambda f, carry: (theirs_of(f, False), carry)[1], 0)
-
+
+    relay_block(3, 0)
     finish(1)
-    relay_on(2, 1, blocks.at[0], blk_r.at[2], 3)
+    relay_block(3, 1)
+    relay_block(2, 0)
+
+    @pl.when(extra)
+    def _():
+        await_extra(1)
+        theirs_of(5, False)
+
     finish(0)
+    relay_block(2, 1)
 
     @pl.when(extra)
     def _():
@@ -271,17 +334,20 @@
         lax.fori_loop(FRAMES, FRAMES + 2, both, 0)
 
     for f in range(FRAMES):
-        slot, when = (6 + f, has_next & not_high) if f < 2 else (f - 2, has_prev)
+        slot, when = (6 + f, has_next & not_high) if f < 2 else (f - 2, not_low)
         arrived(blocks.at[slot], blk_r.at[f], when)
+    for f in (3, 2):
+        for part in range(2):
+            n = 2 * (3 - f) + part
+            arrived(blocks.at[f - 2, pl.ds(HALF * part, HALF)], on_r.at[n], at_low & has_prev)
 
     first, size = bounds[0, 0], bounds[0, 1] - bounds[0, 0]
     offset = first - (t * FRAMES - 2)
-    columns = []
     for j in range(CAP):
         value = blocks[jnp.clip(offset + j, 0, CAP - 1)]
-        columns.append(jnp.where(j < size, value, jnp.zeros_like(value)).astype(F32))
-    out_ref[...] = jnp.stack(columns, axis=1).astype(BF16)
-    for f, when in ((0, None), (4, extra), (5, extra)):
+        slots[:, j, :] = jnp.where(j < size, value, jnp.zeros_like(value)).astype(F32)
+    out_ref[...] = slots[...].astype(BF16)
+    for f, when in ((0, None), (1, None), (4, extra), (5, extra)):
         started.append((send(q_out.at[f], q_in.at[f], q_s.at[f], q_r.at[f], (t, c_far)), when))
         started.append((send(step_out.at[f], step_in.at[f], step_s.at[f], step_r.at[f], (t, c_far)), when))
     for copy, when in started:
@@ -291,24 +357,39 @@
             pl.when(when)(copy.wait_send)
 
 
+def hand_over(held, out_ref, space, in_sems, out_sems):
+    rows = [pl.ds(n * (OWN // PIECES), OWN // PIECES) for n in range(PIECES)]
+    loads = [pltpu.make_async_copy(held.at[r], space.at[r], in_sems.at[n]) for n, r in enumerate(rows)]
+    stores = [pltpu.make_async_copy(space.at[r], out_ref.at[r], out_sems.at[n]) for n, r in enumerate(rows)]
+    for load in loads:
+        load.start()
+    for load, store in zip(loads, stores):
+        load.wait()
+        store.start()
+    for store in stores:
+        store.wait()
+
+
 def shards(latents, conv_weight, norm_gain, norm_bias, clip_lengths, slab_bounds):
-    weights = jnp.transpose(conv_weight, (1, 2, 0, 3)).reshape(TAPS, 512, OWN)
+    weights = jnp.transpose(conv_weight, (1, 2, 0, 3))
     vmem, smem, dma = pltpu.VMEM, pltpu.SMEM, pltpu.SemaphoreType.DMA
-    return pl.pallas_call(
+    held = pl.pallas_call(
         kernel,
         out_shape=jax.ShapeDtypeStruct((OWN, CAP, CELLS), BF16),
         in_specs=[
             pl.BlockSpec(memory_space=smem),
             pl.BlockSpec(memory_space=smem),
-            pl.BlockSpec(memory_space=vmem),
+            pl.BlockSpec(memory_space=pl.ANY),
             pl.BlockSpec(memory_space=pl.ANY),
             pl.BlockSpec(memory_space=vmem),
             pl.BlockSpec(memory_space=vmem),
         ],
         out_specs=pl.BlockSpec(memory_space=vmem),
         scratch_shapes=[
+            vmem((OWN, FRAMES, CELLS), BF16),
+            vmem((OWN, CAP, CELLS), F32),
             vmem((CAP, PAIR, CELLS), BF16),
-            vmem((2, TAPS, 2, OWN, OWN), BF16),
+            vmem((2, 3, 9, 2, OWN, OWN), BF16),
             vmem((MOST, OWN, CELLS), F32),
             vmem((MOST, OWN, CELLS), jnp.int16),
             vmem((MOST, OWN, CELLS), jnp.int16),
@@ -316,15 +397,19 @@
             vmem((MOST, OWN // WIDTH, OWN), F32),
             vmem((CAP, OWN, CELLS), BF16),
             vmem((2, OWN, OWN), F32),
-            vmem((3, OWN, CELLS), BF16),
-            dma((2,)),
-            dma((3,)), dma((3,)),
+            vmem((2, HALF, CELLS), BF16),
+            vmem((4, HALF, CELLS), BF16),
+            dma((3,)),
+            dma((8,)), dma((8,)),
             dma((2,)), dma((2,)),
             dma((2,)), dma((2,)),
             dma((MOST,)), dma((MOST,)),
             dma((MOST,)), dma((MOST,)),
             dma((4,)), dma((4,)),
-            dma((3,)), dma((3,)),
+            dma((2,)), dma((2,)),
+            dma((2,)), dma((2,)),
+            dma((4,)), dma((4,)),
+            dma((4,)), dma((4,)),
             dma((2,)), dma((2,)),
             dma((2,)), dma((2,)),
         ],
@@ -332,6 +417,14 @@
             collective_id=0, has_side_effects=True, vmem_limit_bytes=56 * 2**20
         ),
     )(clip_lengths, slab_bounds, latents, weights, norm_gain.reshape(1, OWN), norm_bias.reshape(1, OWN))
+    return pl.pallas_call(
+        hand_over,
+        out_shape=jax.ShapeDtypeStruct(held.shape, held.dtype),
+        in_specs=[pl.BlockSpec(memory_space=pl.ANY)],
+        out_specs=pl.BlockSpec(memory_space=pl.ANY),
+        scratch_shapes=[vmem((OWN, CAP, CELLS), BF16), dma((PIECES,)), dma((PIECES,))],
+        compiler_params=pltpu.CompilerParams(vmem_limit_bytes=56 * 2**20),
+    )(held)
 
 
 def solution(mesh):

time: 42.5 us -> 41.2 us (0.969); the launches traced: 41.9 us -> 41.1 us
  local copies, waits for them, and re-layouts: 2.26 us -> 0 us
  Pallas kernels: 39.6 us -> 40.9 us
    unnamed x1 -> x0, local copies, waits for them, and re-layouts: 2.26 us -> none
    pallas_call x0 -> x1, Pallas kernels: none -> 1.98 us  [shards(): pl.pallas_call(hand_over, out_shape=jax.ShapeDtypeStruct(held.shape, held...]
    pallas_call x1, Pallas kernels: 39.6 us -> 38.9 us  [shards(): pl.pallas_call(kernel, out_shape=jax.ShapeDtypeStruct((OWN, CAP, CELLS),...]
where the time goes in v4:
time: 41.2 us; the launch traced here: 41.1 us
  Pallas kernels  40.9 us (99%)
    pallas_call x1, Pallas kernels, shards(): pl.pallas_call(kernel, out_shape=jax.ShapeDtypeStruct((OWN, CAP, CELLS),...  38.9 us
    pallas_call x1, Pallas kernels, shards(): pl.pallas_call(hand_over, out_shape=jax.ShapeDtypeStruct(held.shape, held...  1.98 us

profile of v4, /device:TPU:56, one launch (start us, length us, event | category | flops | bytes accessed | tf_op | source)
XLA Modules:
  0.0 41.1 jit_solution(14709846279183083032)
XLA Ops:
  0.0 38.9 %shard_map.64.held = bf16[128,8,512]{2,1,0:T(8,128)(2,1)} custom-call(s32[12]{0:T(128)} %clips.1, s32[1,2]{1,0:T(1,128)} %bounds.1, bf16[128,4,512]{2,1,0:T(4,128)(2,1)} %x_hbm.1, bf16[3,9,512,128]{3,2,1,0:T(8,128)(2,1)} %bitcast.3, f32[1,128]{1,0:T(1,128)} %bitcast.4, f32[1,128]{1,0:T(1,128)} %bitcast.5), custom_call_target="tpu_custom_call" | custom-call | tf_op jit(solution)/shard_map/pallas_call | solution.py:376
  38.9 2.0 %shard_map.65 = bf16[128,8,512]{2,1,0:T(8,128)(2,1)} custom-call(bf16[128,8,512]{2,1,0:T(8,128)(2,1)} %shard_map.64.held), custom_call_target="tpu_custom_call" | custom-call | tf_op jit(solution)/shard_map/pallas_call | solution.py:420

commit v5 on v4

--- a/solution.py
+++ b/solution.py
@@ -21,7 +21,6 @@
 OWN = 128
 PAIR = 256
 HALF = 64
-PIECES = 4
 WIDTH = 512 // GROUPS
 norm_eps = 1e-06
 
@@ -357,25 +356,12 @@
             pl.when(when)(copy.wait_send)
 
 
-def hand_over(held, out_ref, space, in_sems, out_sems):
-    rows = [pl.ds(n * (OWN // PIECES), OWN // PIECES) for n in range(PIECES)]
-    loads = [pltpu.make_async_copy(held.at[r], space.at[r], in_sems.at[n]) for n, r in enumerate(rows)]
-    stores = [pltpu.make_async_copy(space.at[r], out_ref.at[r], out_sems.at[n]) for n, r in enumerate(rows)]
-    for load in loads:
-        load.start()
-    for load, store in zip(loads, stores):
-        load.wait()
-        store.start()
-    for store in stores:
-        store.wait()
-
-
 def shards(latents, conv_weight, norm_gain, norm_bias, clip_lengths, slab_bounds):
     weights = jnp.transpose(conv_weight, (1, 2, 0, 3))
     vmem, smem, dma = pltpu.VMEM, pltpu.SMEM, pltpu.SemaphoreType.DMA
-    held = pl.pallas_call(
+    return pl.pallas_call(
         kernel,
-        out_shape=jax.ShapeDtypeStruct((OWN, CAP, CELLS), BF16),
+        out_shape=vmem((OWN, CAP, CELLS), BF16),
         in_specs=[
             pl.BlockSpec(memory_space=smem),
             pl.BlockSpec(memory_space=smem),
@@ -417,14 +403,6 @@
             collective_id=0, has_side_effects=True, vmem_limit_bytes=56 * 2**20
         ),
     )(clip_lengths, slab_bounds, latents, weights, norm_gain.reshape(1, OWN), norm_bias.reshape(1, OWN))
-    return pl.pallas_call(
-        hand_over,
-        out_shape=jax.ShapeDtypeStruct(held.shape, held.dtype),
-        in_specs=[pl.BlockSpec(memory_space=pl.ANY)],
-        out_specs=pl.BlockSpec(memory_space=pl.ANY),
-        scratch_shapes=[vmem((OWN, CAP, CELLS), BF16), dma((PIECES,)), dma((PIECES,))],
-        compiler_params=pltpu.CompilerParams(vmem_limit_bytes=56 * 2**20),
-    )(held)
 
 
 def solution(mesh):

time: 41.2 us -> 39 us (0.947)
  Pallas kernels: 40.9 us -> 37.9 us
  local copies, waits for them, and re-layouts: 0 us -> 0.97 us
    pallas_call x2 -> x1, Pallas kernels: 40.9 us -> 37.9 us  [shards(): pl.pallas_call(kernel, out_shape=vmem((OWN, CAP, CELLS), BF16), in_specs=...]
    unnamed x0 -> x1, local copies, waits for them, and re-layouts: none -> 0.97 us
where the time goes in v5:
time: 39 us; the launch traced here: 38.9 us
  Pallas kernels  37.9 us (97%)
  local copies, waits for them, and re-layouts  0.97 us (2%)
    pallas_call x1, Pallas kernels, shards(): pl.pallas_call(kernel, out_shape=vmem((OWN, CAP, CELLS), BF16), in_specs=...  37.9 us
    unnamed x1, local copies, waits for them, and re-layouts  0.97 us

profile of v5, /device:TPU:56, one launch (start us, length us, event | category | flops | bytes accessed | tf_op | source)
XLA Modules:
  0.0 38.9 jit_solution(16243671161728070800)
XLA Ops:
  0.0 37.9 %shard_map.64 = bf16[128,8,512]{2,1,0:T(8,128)(2,1)S(1)} custom-call(s32[12]{0:T(128)} %clips.1, s32[1,2]{1,0:T(1,128)} %bounds.1, bf16[128,4,512]{2,1,0:T(4,128)(2,1)} %x_hbm.1, bf16[3,9,512,128]{3,2,1,0:T(8,128)(2,1)} %bitcast.3, f32[1,128]{1,0:T(1,128)} %bitcast.4, f32[1,128]{1,0:T(1,128)} %bitcast.5), custom_call_target="tpu_custom_call" | custom-call | tf_op jit(solution)/shard_map/pallas_call | solution.py:362
  38.0 1.0 %copy.8 = bf16[128,8,512]{2,1,0:T(8,128)(2,1)} copy(bf16[128,8,512]{2,1,0:T(8,128)(2,1)S(1)} %shard_map.64) | data formatting | bytes 2097152

commit v6 on v5

--- a/solution.py
+++ b/solution.py
@@ -153,15 +153,16 @@
 
     for f in (3, 2, 1):
         share_x(f)
-    for a in range(3):
-        share_w(0, pl.ds(3 * a, 3), 4 + a)
-    xn[2, mine, :] = x_ref[:, 0, :]
-    share_x(0)
+    share_w(0, pl.ds(0, 3), 4)
     go(send(xn.at[5, mine], xn.at[1, mine], halo_s.at[1], halo_r.at[1], (t_next, c)), has_next)
     go(send(xn.at[4, mine], xn.at[0, mine], halo_s.at[0], halo_r.at[0], (t_next, c)), has_next & not_high)
     halves = [pl.ds(pl.multiple_of(core * OWN + HALF * part, HALF), HALF) for part in range(2)]
     for part in range(2):
         go(send(xn.at[4, halves[part]], relay.at[part], edge_s.at[part], relay_r.at[part], (slab(-3), c)), has_next & at_high)
+    for a in (1, 2):
+        share_w(0, pl.ds(3 * a, 3), 4 + a)
+    xn[2, mine, :] = x_ref[:, 0, :]
+    share_x(0)
     for h in range(2):
         go(send(xn.at[2 + h, mine], xn.at[6 + h, mine], ext_s.at[h], ext_r.at[h], (t_prev, c)), has_prev & at_low)
 

time: 39 us -> 39 us (level)
  no operation moved by 1% of the time
where the time goes in v6:
time: 39 us; the launch traced here: 38.9 us
  Pallas kernels  37.9 us (97%)
  local copies, waits for them, and re-layouts  0.97 us (2%)
    pallas_call x1, Pallas kernels, shards(): pl.pallas_call(kernel, out_shape=vmem((OWN, CAP, CELLS), BF16), in_specs=...  37.9 us
    unnamed x1, local copies, waits for them, and re-layouts  0.97 us

profile of v6, /device:TPU:56, one launch (start us, length us, event | category | flops | bytes accessed | tf_op | source)
XLA Modules:
  0.0 38.9 jit_solution(10839644616009061340)
XLA Ops:
  0.0 37.9 %shard_map.64 = bf16[128,8,512]{2,1,0:T(8,128)(2,1)S(1)} custom-call(s32[12]{0:T(128)} %clips.1, s32[1,2]{1,0:T(1,128)} %bounds.1, bf16[128,4,512]{2,1,0:T(4,128)(2,1)} %x_hbm.1, bf16[3,9,512,128]{3,2,1,0:T(8,128)(2,1)} %bitcast.3, f32[1,128]{1,0:T(1,128)} %bitcast.4, f32[1,128]{1,0:T(1,128)} %bitcast.5), custom_call_target="tpu_custom_call" | custom-call | tf_op jit(solution)/shard_map/pallas_call | solution.py:363
  37.9 1.0 %copy.8 = bf16[128,8,512]{2,1,0:T(8,128)(2,1)} copy(bf16[128,8,512]{2,1,0:T(8,128)(2,1)S(1)} %shard_map.64) | data formatting | bytes 2097152
